TPU v7x, 32 devices: a whole 2x2x4 slice. The times are simulated.
32 devices in a mesh: groups: 2 (over y), dp: 8 (over z, x), feat: 2 (over core).
Axes of the slice: x: 2, y: 2, z: 4, core: 2. Of those that a mesh axis runs over, the one named last changes fastest.
Arguments:
- frames: float32 [262144, 128], P(('groups', 'dp', 'feat')), parts along dimension 0, may hold values from -6 to 6
- pivots: int32 [4, 128], P('groups'), parts along dimension 0, may hold values from 0 to 131071, as said below
Outputs:
- factor: float32 [262144, 256], P(('groups', 'dp', 'feat')), parts along dimension 0
- residual_diag: float32 [262144], P(('groups', 'dp', 'feat')), parts along dimension 0
There are 2 independent parts, one for each index of `groups`. A program takes and returns all parts, laid end to end along the dimension named above; each array names one. Nothing has to cross between parts.
Inputs may be any that keep to these rules, and one draw needn't show every extreme that they name: `pivots`: each row holds 128 distinct frame ids and no id is in both rows. Frame f lies on the device at index f // 8192 along dp+feat. At most 32 ids of one row lie on one device, and in every row some device holds exactly 32.
All inputs are finite; a program needn't handle non-finite values.
Results may differ from a plain program's by a relative error of at most 0.0003.
Values sent between devices are 32-bit elements; how exact they have to be, the bound alone decides.
A program may use at most 64 MiB of HBM per device.

v0:
```python
import jax
import jax.numpy as jnp
from jax import lax
from jax.sharding import PartitionSpec as P


def kernel_block(left, right):
    products = jnp.dot(
        left, right.T, precision=lax.Precision.HIGHEST, preferred_element_type=jnp.float32
    )
    left_sq = jnp.sum(left * left, axis=1)
    right_sq = jnp.sum(right * right, axis=1)
    distance = left_sq[:, None] + right_sq[None, :] - 2.0 * products
    return jnp.exp(distance * (-0.5 / left.shape[1]))


def lower_inverse(pivot_block):
    lower_part = jnp.linalg.cholesky(pivot_block)
    identity = jnp.eye(pivot_block.shape[0], dtype=pivot_block.dtype)
    return jax.scipy.linalg.solve_triangular(lower_part, identity, lower=True)


def apply_inverse(columns, inverse):
    return jnp.dot(
        columns, inverse.T, precision=lax.Precision.HIGHEST, preferred_element_type=jnp.float32
    )


def masked_rows(table, pivot_ids, row_start, row_count):
    is_mine = (pivot_ids >= row_start) & (pivot_ids < row_start + row_count)
    local_rows = jnp.where(is_mine, pivot_ids - row_start, 0)
    return jnp.where(is_mine[:, None], table[local_rows], 0.0)


def shards(frames, pivots):
    row_count = frames.shape[0]
    my_index = lax.axis_index(("dp", "feat"))
    row_start = my_index * row_count
    first_ids = pivots[0]
    second_ids = pivots[1]
    first_points = lax.psum(masked_rows(frames, first_ids, row_start, row_count), ("dp", "feat"))
    first_inverse = lower_inverse(kernel_block(first_points, first_points))
    first_factor = apply_inverse(kernel_block(frames, first_points), first_inverse)
    second_points, earlier_rows = lax.psum(
        (
            masked_rows(frames, second_ids, row_start, row_count),
            masked_rows(first_factor, second_ids, row_start, row_count),
        ),
        ("dp", "feat"),
    )
    columns = kernel_block(frames, second_points) - jnp.dot(
        first_factor,
        earlier_rows.T,
        precision=lax.Precision.HIGHEST,
        preferred_element_type=jnp.float32,
    )
    pivot_block = kernel_block(second_points, second_points) - jnp.dot(
        earlier_rows,
        earlier_rows.T,
        precision=lax.Precision.HIGHEST,
        preferred_element_type=jnp.float32,
    )
    second_factor = apply_inverse(columns, lower_inverse(pivot_block))
    residual_diag = 1.0 - jnp.sum(first_factor * first_factor, axis=1)
    residual_diag = residual_diag - jnp.sum(second_factor * second_factor, axis=1)
    return (jnp.concatenate([first_factor, second_factor], axis=1), residual_diag)


def solution(mesh):
    placed = (P(("groups", "dp", "feat"), None), P("groups", None))
    return jax.shard_map(
        shards,
        mesh=mesh,
        in_specs=placed,
        out_specs=(P(("groups", "dp", "feat"), None), P(("groups", "dp", "feat"))),
        check_vma=False,
    )
```

profile of v0, /device:TPU:0, one launch (start us, length us, event | category | flops | bytes accessed | tf_op | source)
XLA Modules:
  0.0 301.4 jit_solution(100093732987892)
XLA Ops:
  7.2 0.8 fusion.26
  8.0 0.8 fusion.24
  8.8 2.8 gather_fusion
  11.6 0.7 broadcast_select_fusion.2
  12.4 3.3 %multiply_reduce_fusion.2 = f32[8192]{0:T(1024)S(1)} fusion(f32[8192,128]{1,0:T(8,128)} %param.5), kind=kLoop, calls=%fused_computation.17 | loop fusion | flops 2088960 | bytes 4227072 | tf_op jit(solution)/shard_map/reduce_sum | solution.py:11
  15.7 2.8 gather_fusion.1
  18.6 81.0 %all-reduce.4.cloned.1.call-done = f32[128,128]{1,0:T(8,128)} async-done(((f32[128,128]{1,0:T(8,128)}), f32[128,128]{1,0:T(8,128)}) %all-reduce.4.cloned.1.call-update) | async-done | bytes 65552 | tf_op jit(solution)/shard_map/psum | solution.py:41
  99.5 0.9 multiply_reduce_fusion.4
  100.5 1.2 fusion.13
  101.8 11.7 %cholesky.44 = f32[128,128]{1,0:T(8,128)S(1)} custom-call(f32[128,128]{1,0:T(8,128)S(1)} %fusion.23), custom_call_target="Cholesky" | custom-call | tf_op jit(solution)/shard_map/jit(cholesky)/cholesky | solution.py:18
  113.6 0.6 compare_reduce_fusion.1
  114.2 0.7 fusion.18
  114.9 9.8 %custom-call.6 = f32[1,128,128]{1,2,0:T(8,128)S(1)} custom-call(f32[1,128,128]{2,1,0:T(8,128)S(1)} %fusion.18), custom_call_target="InvertDiagBlocksLowerTriangular" | custom-call | tf_op jit(solution)/shard_map/jit(_solve_triangular)/triangular_solve | solution.py:20
  125.0 6.3 %fusion.7 = f32[8192,128]{1,0:T(8,128)S(1)} fusion(f32[128,128]{1,0:T(8,128)} %all-reduce.4.cloned.1.call-done, f32[8192,128]{1,0:T(8,128)} %param.5, f32[128]{0:T(128)S(1)} %multiply_reduce_fusion.4, f32[8192]{0:T(1024)S(1)} %multiply_reduce_fusion.2), kind=kOutput, calls=%fused_computation.13 | convolution fusion | flops 1614807040 | bytes 8487424 | tf_op jit(solution)/shard_map/dot_general | solution.py:8
  131.2 5.5 %multiply_reduce_fusion.1 = (f32[8192]{0:T(1024)S(1)}, f32[8192,128]{0,1:T(8,128)}) fusion(f32[8192,128]{1,0:T(8,128)S(1)} %fusion.7, f32[128,128]{1,0:T(8,128)S(1)} %fusion.16), kind=kOutput, calls=%fused_computation.16 | convolution fusion | flops 1612701696 | bytes 8486912 | tf_op jit(solution)/shard_map/dot_general | solution.py:24
  136.8 5.6 %copy.6 = f32[8192,128]{1,0:T(8,128)} copy(f32[8192,128]{0,1:T(8,128)} %get-tuple-element.17) | data formatting | bytes 8388608 | tf_op jit(solution)/shard_map/dot_general | solution.py:24
  142.3 2.8 gather_fusion.2
  145.1 0.7 broadcast_select_fusion
  145.9 88.8 %all-reduce.6.cloned.1.call-done = (f32[128,128]{1,0:T(8,128)}, f32[128,128]{1,0:T(8,128)}) async-done(((f32[128,128]{1,0:T(8,128)}, f32[128,128]{1,0:T(8,128)}), (f32[128,128]{1,0:T(8,128)}, f32[128,128]{1,0:T(8,128)})) %all-reduce.6.cloned.1.call-update) | async-done | bytes 131088 | tf_op jit(solution)/shard_map/psum | solution.py:44
  234.7 0.9 multiply_reduce_fusion.3
  235.6 1.2 fusion.10
  236.9 7.1 %fusion.3 = f32[8192,128]{1,0:T(8,128)} fusion(f32[128,128]{1,0:T(8,128)} %get-tuple-element.6, f32[8192,128]{1,0:T(8,128)} %param.5, f32[128]{0:T(128)S(1)} %multiply_reduce_fusion.3, f32[8192]{0:T(1024)S(1)} %multiply_reduce_fusion.2), kind=kOutput, calls=%fused_computation.8 | convolution fusion | flops 1614807040 | bytes 8487424 | tf_op jit(solution)/shard_map/dot_general | solution.py:8
  244.4 11.7 %cholesky.55 = f32[128,128]{1,0:T(8,128)S(1)} custom-call(f32[128,128]{1,0:T(8,128)S(1)} %fusion.21), custom_call_target="Cholesky" | custom-call | tf_op jit(solution)/shard_map/jit(cholesky)/cholesky | solution.py:18
  256.1 0.6 compare_reduce_fusion
  256.8 0.7 fusion.19
  257.4 9.8 %custom-call.7 = f32[1,128,128]{1,2,0:T(8,128)S(1)} custom-call(f32[1,128,128]{2,1,0:T(8,128)S(1)} %fusion.19), custom_call_target="InvertDiagBlocksLowerTriangular" | custom-call | tf_op jit(solution)/shard_map/jit(_solve_triangular)/triangular_solve | solution.py:20
  267.2 0.3 fusion.14
  267.5 9.5 %convolution_subtract_fusion = f32[8192,128]{1,0:T(8,128)S(1)} fusion(f32[8192,128]{1,0:T(8,128)} %fusion.3, f32[8192,128]{0,1:T(8,128)} %get-tuple-element.17, f32[128,128]{1,0:T(8,128)S(1)} %copy-done.1), kind=kOutput, calls=%fused_computation.3 | convolution fusion | flops 1611661312 | bytes 12648448 | tf_op jit(solution)/shard_map/dot_general | solution.py:51
  277.1 4.1 %multiply_reduce_fusion = (f32[8192]{0:T(1024)S(1)}, f32[8192,128]{0,1:T(8,128)S(1)}) fusion(f32[8192,128]{1,0:T(8,128)S(1)} %convolution_subtract_fusion, f32[128,128]{1,0:T(8,128)S(1)} %fusion.14), kind=kOutput, calls=%fused_computation.15 | convolution fusion | flops 1612701696 | bytes 8486912 | tf_op jit(solution)/shard_map/dot_general | solution.py:24
  281.2 3.8 %pad_maximum_fusion = f32[8192,256]{0,1:T(8,128)} fusion(f32[8192,128]{0,1:T(8,128)S(1)} %get-tuple-element.15, f32[8192,128]{0,1:T(8,128)S(1)} %copy-done), kind=kLoop, calls=%fused_computation.14 | loop fusion | flops 2097152 | bytes 16777216 | tf_op jit(solution)/shard_map/concatenate | solution.py:66
  285.0 9.0 %copy.10 = f32[8192,256]{1,0:T(8,128)} copy(f32[8192,256]{0,1:T(8,128)} %pad_maximum_fusion) | data formatting | bytes 16777216
  294.0 0.6 subtract_subtract_fusion
  (17 shorter events, 1.0 us)
Async XLA Ops:
  7.2 92.4 %all-reduce.4.cloned.1.call-start = ((), (), s32[]{:S(2)}) async-start(), calls=%async_computation | async-start | bytes 131072 | tf_op jit(solution)/shard_map/psum | solution.py:41
  12.3 222.4 %all-reduce.6.cloned.1.call-start = ((), (), s32[]{:S(2)}) async-start(), calls=%async_computation.1 | async-start | bytes 262144 | tf_op jit(solution)/shard_map/psum | solution.py:44
  236.9 7.1 %copy-start.1 = (f32[128,128]{1,0:T(8,128)S(1)}, f32[128,128]{1,0:T(8,128)}, u32[]{:S(2)}) copy-start(f32[128,128]{1,0:T(8,128)} %get-tuple-element.7) | copy-start | bytes 196612
  277.1 4.1 %copy-start = (f32[8192,128]{0,1:T(8,128)S(1)}, f32[8192,128]{0,1:T(8,128)}, u32[]{:S(2)}) copy-start(f32[8192,128]{0,1:T(8,128)} %get-tuple-element.17) | copy-start | bytes 12582916
Sparse Core Ops, SparseCore 0:
  12.4 87.0 all-reduce.3
  146.0 88.6 all-reduce.5
where the time goes:
time: 303 us; the launch traced here: 301 us
  waiting for transfers between devices  170 us (56%)
  other arithmetic  58.3 us (19%)
  matrix products  35.7 us (12%)
  local copies, waits for them, and re-layouts  23.2 us (8%)
  between operations  14.2 us (5%)
    psum x1, waiting for transfers between devices, shards(): lax.psum((masked_rows(frames, second_ids, row_start, row_count), masked_r...  88.8 us
    psum x1, waiting for transfers between devices, shards(): lax.psum(masked_rows(frames, first_ids, row_start, row_count), ('dp', 'fe...  81 us
    another operation x6, other arithmetic, lower_inverse(): lower_part = jnp.linalg.cholesky(pivot_block)  24.8 us
    another operation x4, other arithmetic, lower_inverse(): return jax.scipy.linalg.solve_triangular(lower_part, identity, lower=True)  20.9 us
    dot_general x4, matrix products, kernel_block(): jnp.dot(left, right.T, precision=lax.Precision.HIGHEST, preferred_element...  15.8 us
    dot_general x2, matrix products, apply_inverse(): jnp.dot(columns, inverse.T, precision=lax.Precision.HIGHEST, preferred_el...  9.58 us
    dot_general x1, matrix products, shards(): jnp.dot(first_factor, earlier_rows.T, precision=lax.Precision.HIGHEST, pr...  9.54 us
    unnamed x5, local copies, waits for them, and re-layouts  9 us
  transfers between devices with their start and end apart: 2, of which 2 were waited for; matrix products, arithmetic and copies ran while one was open for 2% of the time, Pallas kernels for 0%

commit v1 on v0

v1 whole, which is shorter than its diff:
```python
import functools

import jax
import jax.numpy as jnp
from jax import lax
from jax.experimental import pallas as pl
from jax.experimental.pallas import tpu as pltpu
from jax.sharding import PartitionSpec as P

HIGHEST = lax.Precision.HIGHEST
MESH = pl.DeviceIdType.MESH
SUB = 8
TILE = 1024


def gather_kernel(count, feat_size, pivots, frames, points, held, mine, came, full, load_sem, s1, r1, s2, r2):
    me = lax.axis_index("dp") * feat_size + lax.axis_index("feat")
    row_count = frames.shape[0]
    start = me * row_count
    share = mine.shape[1]
    block = pivots.shape[1]

    load = pltpu.make_async_copy(frames, held, load_sem)
    load.start()

    def device(index):
        return {"dp": index // feat_size, "feat": index % feat_size}

    barrier = pltpu.get_barrier_semaphore()

    def greet(step, carry):
        other = lax.rem(me + step, count)
        pl.semaphore_signal(barrier, inc=1, device_id=device(other), device_id_type=MESH)
        return carry

    lax.fori_loop(1, count, greet, 0)
    load.wait()

    def pick(owner, carry):
        for k in range(share):
            slot = owner * share + k
            local = pivots[slot // block, slot % block] - start
            is_mine = (local >= 0) & (local < row_count)
            row = held[pl.ds(jnp.clip(local, 0, row_count - 1), 1), :]
            mine[owner, pl.ds(k, 1), :] = row * jnp.where(is_mine, 1.0, 0.0)
        return carry

    lax.fori_loop(0, count, pick, 0)
    pl.semaphore_wait(barrier, count - 1)

    def collect(step):
        other = lax.rem(me + step, count)
        return pltpu.make_async_remote_copy(
            src_ref=mine.at[other],
            dst_ref=came.at[step],
            send_sem=s1.at[step],
            recv_sem=r1.at[step],
            device_id=device(other),
            device_id_type=MESH,
        )

    def spread(step):
        other = lax.rem(me + step, count)
        return pltpu.make_async_remote_copy(
            src_ref=full.at[me],
            dst_ref=full.at[me],
            send_sem=s2.at[step],
            recv_sem=r2.at[step],
            device_id=device(other),
            device_id_type=MESH,
        )

    def spread_arrival(step):
        source = lax.rem(me + count - step, count)
        return pltpu.make_async_remote_copy(
            src_ref=full.at[source],
            dst_ref=full.at[source],
            send_sem=s2.at[step],
            recv_sem=r2.at[step],
            device_id=device(source),
            device_id_type=MESH,
        )

    def run(action):
        def body(step, carry):
            action(step)
            return carry

        lax.fori_loop(1, count, body, 0)

    run(lambda step: collect(step).start())

    def add(step, total):
        collect(step).wait_recv()
        return total + came[step]

    full[me] = lax.fori_loop(1, count, add, mine[me])
    run(lambda step: spread(step).start())
    run(lambda step: spread_arrival(step).wait_recv())
    run(lambda step: collect(step).wait_send())
    run(lambda step: spread(step).wait_send())
    points[...] = full[...]


def gather_points(mesh, frames, pivots):
    count = mesh.shape["dp"] * mesh.shape["feat"]
    blocks, block = pivots.shape
    slots = blocks * block
    share = slots // count
    feat = frames.shape[1]
    table = (count, share, feat)
    sems = pltpu.SemaphoreType.DMA((count,))
    points = pl.pallas_call(
        functools.partial(gather_kernel, count, mesh.shape["feat"]),
        out_shape=jax.ShapeDtypeStruct(table, jnp.float32),
        in_specs=[pl.BlockSpec(memory_space=pltpu.SMEM), pl.BlockSpec(memory_space=pl.ANY)],
        out_specs=pl.BlockSpec(memory_space=pltpu.VMEM),
        scratch_shapes=[
            pltpu.VMEM(frames.shape, jnp.float32),
            pltpu.VMEM(table, jnp.float32),
            pltpu.VMEM(table, jnp.float32),
            pltpu.VMEM(table, jnp.float32),
            pltpu.SemaphoreType.DMA(()),
            sems,
            sems,
            sems,
            sems,
        ],
        compiler_params=pltpu.CompilerParams(
            collective_id=0, has_side_effects=True, vmem_limit_bytes=16 * 1024 * 1024
        ),
    )(pivots, frames)
    return points.reshape(slots, feat)


def dot(left, right, dims=((1,), (0,)), precision=None):
    return lax.dot_general(
        left, right, (dims, ((), ())), precision=precision, preferred_element_type=jnp.float32
    )


def halves(value):
    high = value.astype(jnp.bfloat16)
    return high, (value - high.astype(jnp.float32)).astype(jnp.bfloat16)


def inverse_factor(matrix):
    size = matrix.shape[0]
    rows = [matrix[i * SUB : (i + 1) * SUB, :] for i in range(size // SUB)]
    sub = lax.broadcasted_iota(jnp.int32, (SUB, size), 0)
    lane = lax.broadcasted_iota(jnp.int32, (SUB, size), 1)

    def column(value, index):
        return jnp.broadcast_to(value[:, index : index + 1], (SUB, size))

    def row(value, index):
        return jnp.broadcast_to(value[index : index + 1, :], (SUB, size))

    out = []
    for k in range(size // SUB):
        base = k * SUB
        in_block = (lane >= base) & (lane < base + SUB)
        cols = [column(rows[k], base + j) for j in range(SUB)]
        work = jnp.where(in_block, jnp.where(lane - base == sub, 1.0, 0.0), rows[k])
        done = jnp.zeros((SUB, size), jnp.float32)
        for j in range(SUB):
            pivot = row(cols[j], j)
            inverse = 1.0 / pivot
            pivot_row = row(work, j)
            done = jnp.where(sub == j, pivot_row * lax.rsqrt(pivot), done)
            scaled = cols[j] * inverse
            work = jnp.where(sub == j, pivot_row * inverse, work - scaled * pivot_row)
            for m in range(j + 1, SUB):
                pivot_col = row(cols[m], j)
                cols[m] = jnp.where(sub == j, pivot_col * inverse, cols[m] - scaled * pivot_col)
        out.append(jnp.where(lane <= base + sub, done, 0.0))
        reduced = [row(work, j) for j in range(SUB)]
        for i in range(k + 1, size // SUB):
            update = [column(rows[i], base + j) * reduced[j] for j in range(SUB)]
            while len(update) > 1:
                update = [a + b for a, b in zip(update[::2], update[1::2])]
            rows[i] = jnp.where(in_block, 0.0, rows[i]) - update[0]
    return jnp.concatenate(out, axis=0)


def factor_kernel(points, frames, factor, residual, pts_hi, pts_lo, norms, wt_hi, wt_lo):
    feat = points.shape[1]
    block = points.shape[0] // 2
    scale = -0.5 / feat

    @pl.when(pl.program_id(0) == 0)
    def _():
        pts = points[...]
        squares = pts * pts
        ones = jnp.ones((SUB, feat), jnp.float32)
        row_norms = dot(ones, squares, ((1,), (1,)), HIGHEST)
        norms[...] = row_norms
        products = dot(pts, pts, ((1,), (1,)), HIGHEST)
        gram = jnp.exp(
            (jnp.sum(squares, axis=1, keepdims=True) + row_norms[:1] - 2.0 * products) * scale
        )
        first = inverse_factor(gram[:block, :block])
        earlier = dot(gram[block:, :block], first, ((1,), (1,)), HIGHEST)
        second = inverse_factor(
            gram[block:, block:] - dot(earlier, earlier, ((1,), (1,)), HIGHEST)
        )
        mixed = -dot(second, dot(earlier, first, precision=HIGHEST), precision=HIGHEST)
        whole = jnp.concatenate(
            [
                jnp.concatenate([first, jnp.zeros_like(first)], axis=1),
                jnp.concatenate([mixed, second], axis=1),
            ],
            axis=0,
        ).T
        high, low = halves(whole)
        wt_hi[...] = high
        wt_lo[...] = low
        high, low = halves(pts.T)
        pts_hi[...] = high
        pts_lo[...] = low

    tile = frames[...]
    tile_norms = jnp.sum(tile * tile, axis=1, keepdims=True)
    high, low = halves(tile)
    both = jnp.concatenate([high, low], axis=1)
    products = dot(both, jnp.concatenate([pts_hi[...]] * 2, axis=0)) + dot(high, pts_lo[...])
    kern = jnp.exp((tile_norms + norms[:1] - 2.0 * products) * scale)
    high, low = halves(kern)
    result = dot(high, wt_hi[...]) + dot(low, wt_hi[...]) + dot(high, wt_lo[...])
    factor[...] = result
    high, low = halves(result * result)
    ones = jnp.ones((SUB, result.shape[1]), jnp.bfloat16)
    sums = dot(ones, high, ((1,), (1,))) + dot(ones, low, ((1,), (1,)))
    residual[0] = 1.0 - sums[:1]


def shards(mesh, frames, pivots):
    points = gather_points(mesh, frames, pivots)
    row_count, feat = frames.shape
    slots = points.shape[0]
    tiles = row_count // TILE
    factor, residual = pl.pallas_call(
        factor_kernel,
        grid=(tiles,),
        out_shape=(
            jax.ShapeDtypeStruct((row_count, slots), jnp.float32),
            jax.ShapeDtypeStruct((tiles, 1, TILE), jnp.float32),
        ),
        in_specs=[
            pl.BlockSpec((slots, feat), lambda i: (0, 0)),
            pl.BlockSpec((TILE, feat), lambda i: (i, 0)),
        ],
        out_specs=(
            pl.BlockSpec((TILE, slots), lambda i: (i, 0)),
            pl.BlockSpec((1, 1, TILE), lambda i: (i, 0, 0)),
        ),
        scratch_shapes=[
            pltpu.VMEM((feat, slots), jnp.bfloat16),
            pltpu.VMEM((feat, slots), jnp.bfloat16),
            pltpu.VMEM((SUB, slots), jnp.float32),
            pltpu.VMEM((slots, slots), jnp.bfloat16),
            pltpu.VMEM((slots, slots), jnp.bfloat16),
        ],
        compiler_params=pltpu.CompilerParams(vmem_limit_bytes=40 * 1024 * 1024),
    )(points, frames)
    return factor, residual.reshape(row_count)


def solution(mesh):
    placed = (P(("groups", "dp", "feat"), None), P("groups", None))
    return jax.shard_map(
        functools.partial(shards, mesh),
        mesh=mesh,
        in_specs=placed,
        out_specs=(P(("groups", "dp", "feat"), None), P(("groups", "dp", "feat"))),
        check_vma=False,
    )
```

time: 303 us -> 48.8 us (0.16)
  waiting for transfers between devices: 170 us -> 0 us
  other arithmetic: 58.3 us -> 0 us
  Pallas kernels: 0 us -> 42.9 us
  matrix products: 35.7 us -> 0 us
  local copies, waits for them, and re-layouts: 23.2 us -> 5.04 us
  between operations: 14.2 us -> 0.66 us
    psum x2 -> x0, waiting for transfers between devices: 170 us -> none  [the longest x1 88.8 us: shards(): lax.psum((masked_rows(frames, second_ids, row_start, row_count), masked_r...]
    another operation x10 -> x0, other arithmetic: 45.7 us -> none  [the longest x6 24.8 us: lower_inverse(): lower_part = jnp.linalg.cholesky(pivot_block)]
    pallas_call x0 -> x2, Pallas kernels: none -> 42.9 us  [the longest x1 25.7 us: shards(): pl.pallas_call(factor_kernel, grid=(tiles,), out_shape=(jax.ShapeDtypeStr...]
    dot_general x8 -> x0, matrix products: 35.2 us -> none  [the longest x4 15.8 us: kernel_block(): jnp.dot(left, right.T, precision=lax.Precision.HIGHEST, preferred_element...]
    gather x3 -> x0, local copies, waits for them, and re-layouts: 8.5 us -> none  [masked_rows(): return jnp.where(is_mine[:, None], table[local_rows], 0.0)]
    dot_general x1 -> x0, local copies, waits for them, and re-layouts: 5.57 us -> none  [apply_inverse(): jnp.dot(columns, inverse.T, precision=lax.Precision.HIGHEST, preferred_el...]
    reduce_sum x3 -> x0, other arithmetic: 5.22 us -> none  [the longest x1 3.34 us: kernel_block(): left_sq = jnp.sum(left * left, axis=1)]
    unnamed x5 -> x6, local copies, waits for them, and re-layouts: 9 us -> 5.04 us
  transfers between devices with their start and end apart: 2 -> 0, of which waited for: 2 -> 0; matrix products, arithmetic and copies ran while one was open for 2% -> 0% of each run, Pallas kernels for 0% -> 0%
where the time goes in v1:
time: 48.8 us; the launch traced here: 48.6 us
  Pallas kernels  42.9 us (88%)
  local copies, waits for them, and re-layouts  5.04 us (10%)
  between operations  0.66 us (1%)
    pallas_call x1, Pallas kernels, shards(): pl.pallas_call(factor_kernel, grid=(tiles,), out_shape=(jax.ShapeDtypeStr...  25.7 us
    pallas_call x1, Pallas kernels, gather_points(): pl.pallas_call(functools.partial(gather_kernel, count, mesh.shape['feat']...  17.2 us
    unnamed x6, local copies, waits for them, and re-layouts  5.04 us

profile of v1, /device:TPU:0, one launch (start us, length us, event | category | flops | bytes accessed | tf_op | source)
XLA Modules:
  0.0 48.6 jit_solution(5964993050264597920)
XLA Ops:
  0.6 0.0 copy-start
  0.6 2.2 %copy-done = f32[8192,128]{1,0:T(8,128)S(1)} copy-done((f32[8192,128]{1,0:T(8,128)S(1)}, f32[8192,128]{1,0:T(8,128)}, u32[]{:S(2)}) %copy-start) | copy-done | bytes 4194328
  2.8 0.0 copy-start.2
  2.8 0.7 %copy-done.2 = s32[2,128]{1,0:T(2,128)S(1)} copy-done((s32[2,128]{1,0:T(2,128)S(1)}, s32[2,128]{1,0:T(2,128)}, u32[]{:S(2)}) %copy-start.2) | copy-done | bytes 1048
  3.5 17.2 %shard_map.41 = f32[16,16,128]{2,1,0:T(8,128)S(1)} custom-call(s32[2,128]{1,0:T(2,128)S(1)} %copy-done.2, f32[8192,128]{1,0:T(8,128)S(1)} %copy-done), custom_call_target="tpu_custom_call" | custom-call | tf_op jit(solution)/shard_map/pallas_call | solution.py:113
  20.7 0.0 copy-start.1
  20.7 2.2 %copy-done.1 = f32[8192,128]{1,0:T(8,128)S(1)} copy-done((f32[8192,128]{1,0:T(8,128)S(1)}, f32[8192,128]{1,0:T(8,128)}, u32[]{:S(2)}) %copy-start.1) | copy-done | bytes 4194328
  22.9 25.7 %shard_map.42 = (f32[8192,256]{1,0:T(8,128)}, f32[8,1,1024]{2,1,0:T(1,128)}) custom-call(f32[256,128]{1,0:T(8,128)S(1)} %bitcast.2, f32[8192,128]{1,0:T(8,128)S(1)} %copy-done.1), custom_call_target="tpu_custom_call" | custom-call | tf_op jit(solution)/shard_map/pallas_call | solution.py:242
Async XLA Ops:
  0.6 2.2 %copy-start = (f32[8192,128]{1,0:T(8,128)S(1)}, f32[8192,128]{1,0:T(8,128)}, u32[]{:S(2)}) copy-start(f32[8192,128]{1,0:T(8,128)} %frames.3) | copy-start | bytes 12582916
  2.8 0.7 %copy-start.2 = (s32[2,128]{1,0:T(2,128)S(1)}, s32[2,128]{1,0:T(2,128)}, u32[]{:S(2)}) copy-start(s32[2,128]{1,0:T(2,128)} %pivots.1) | copy-start | bytes 3076
  20.7 2.2 %copy-start.1 = (f32[8192,128]{1,0:T(8,128)S(1)}, f32[8192,128]{1,0:T(8,128)}, u32[]{:S(2)}) copy-start(f32[8192,128]{1,0:T(8,128)} %frames.3) | copy-start | bytes 12582916

commit v2 on v1

--- a/solution.py
+++ b/solution.py
@@ -1,4 +1,5 @@
 import functools
+import math
 
 import jax
 import jax.numpy as jnp
@@ -127,7 +128,7 @@
             sems,
         ],
         compiler_params=pltpu.CompilerParams(
-            collective_id=0, has_side_effects=True, vmem_limit_bytes=16 * 1024 * 1024
+            collective_id=0, has_side_effects=True, vmem_limit_bytes=60 * 1024 * 1024
         ),
     )(pivots, frames)
     return points.reshape(slots, feat)
@@ -183,21 +184,21 @@
     return jnp.concatenate(out, axis=0)
 
 
-def factor_kernel(points, frames, factor, residual, pts_hi, pts_lo, norms, wt_hi, wt_lo):
+def factor_kernel(points, frames, factor, residual, pts, wt):
     feat = points.shape[1]
-    block = points.shape[0] // 2
-    scale = -0.5 / feat
+    slots = points.shape[0]
+    block = slots // 2
+    fold = -0.5 / feat * math.log2(math.e)
 
     @pl.when(pl.program_id(0) == 0)
     def _():
-        pts = points[...]
-        squares = pts * pts
+        table = points[...]
+        squares = table * table
         ones = jnp.ones((SUB, feat), jnp.float32)
-        row_norms = dot(ones, squares, ((1,), (1,)), HIGHEST)
-        norms[...] = row_norms
-        products = dot(pts, pts, ((1,), (1,)), HIGHEST)
-        gram = jnp.exp(
-            (jnp.sum(squares, axis=1, keepdims=True) + row_norms[:1] - 2.0 * products) * scale
+        norms = fold * dot(ones, squares, ((1,), (1,)), HIGHEST)
+        products = dot(table, table, ((1,), (1,)), HIGHEST)
+        gram = jnp.exp2(
+            (fold * jnp.sum(squares, axis=1, keepdims=True) + norms[:1]) - 2.0 * fold * products
         )
         first = inverse_factor(gram[:block, :block])
         earlier = dot(gram[block:, :block], first, ((1,), (1,)), HIGHEST)
@@ -213,25 +214,34 @@
             axis=0,
         ).T
         high, low = halves(whole)
-        wt_hi[...] = high
-        wt_lo[...] = low
-        high, low = halves(pts.T)
-        pts_hi[...] = high
-        pts_lo[...] = low
+        wt[...] = jnp.concatenate([high, high, low], axis=0)
+        high, low = halves((-2.0 * fold) * table.T)
+        n_high, n_rest = halves(norms)
+        rest = norms - n_high.astype(jnp.float32)
+        n_low = (rest - n_rest.astype(jnp.float32)).astype(jnp.bfloat16)
+        row = lax.broadcasted_iota(jnp.int32, (feat, slots), 0)
+        extra = jnp.where(
+            row == 0,
+            n_high[:1].astype(jnp.float32),
+            jnp.where(
+                row == 1,
+                n_rest[:1].astype(jnp.float32),
+                jnp.where(row == 2, n_low[:1].astype(jnp.float32), 0.0),
+            ),
+        ).astype(jnp.bfloat16)
+        pts[...] = jnp.concatenate([high, high, low, extra], axis=0)
 
     tile = frames[...]
-    tile_norms = jnp.sum(tile * tile, axis=1, keepdims=True)
+    tile_norms = fold * jnp.sum(tile * tile, axis=1, keepdims=True)
     high, low = halves(tile)
-    both = jnp.concatenate([high, low], axis=1)
-    products = dot(both, jnp.concatenate([pts_hi[...]] * 2, axis=0)) + dot(high, pts_lo[...])
-    kern = jnp.exp((tile_norms + norms[:1] - 2.0 * products) * scale)
-    high, low = halves(kern)
-    result = dot(high, wt_hi[...]) + dot(low, wt_hi[...]) + dot(high, wt_lo[...])
+    exponent = dot(
+        jnp.concatenate([high, low, high, jnp.ones_like(high)], axis=1), pts[...]
+    )
+    high, low = halves(jnp.exp2(tile_norms + exponent))
+    result = dot(jnp.concatenate([high, low, high], axis=1), wt[...])
     factor[...] = result
-    high, low = halves(result * result)
-    ones = jnp.ones((SUB, result.shape[1]), jnp.bfloat16)
-    sums = dot(ones, high, ((1,), (1,))) + dot(ones, low, ((1,), (1,)))
-    residual[0] = 1.0 - sums[:1]
+    squares = result[:, :block] * result[:, :block] + result[:, block:] * result[:, block:]
+    residual[0] = 1.0 - jnp.sum(squares.T, axis=0, keepdims=True)
 
 
 def shards(mesh, frames, pivots):
@@ -255,13 +265,10 @@
             pl.BlockSpec((1, 1, TILE), lambda i: (i, 0, 0)),
         ),
         scratch_shapes=[
-            pltpu.VMEM((feat, slots), jnp.bfloat16),
-            pltpu.VMEM((feat, slots), jnp.bfloat16),
-            pltpu.VMEM((SUB, slots), jnp.float32),
-            pltpu.VMEM((slots, slots), jnp.bfloat16),
-            pltpu.VMEM((slots, slots), jnp.bfloat16),
+            pltpu.VMEM((4 * feat, slots), jnp.bfloat16),
+            pltpu.VMEM((3 * slots, slots), jnp.bfloat16),
         ],
-        compiler_params=pltpu.CompilerParams(vmem_limit_bytes=40 * 1024 * 1024),
+        compiler_params=pltpu.CompilerParams(vmem_limit_bytes=60 * 1024 * 1024),
     )(points, frames)
     return factor, residual.reshape(row_count)
 

time: 48.8 us -> 44.7 us (0.916)
  local copies, waits for them, and re-layouts: 5.04 us -> 0 us
  Pallas kernels: 42.9 us -> 43.9 us
    unnamed x6 -> x0, local copies, waits for them, and re-layouts: 5.04 us -> none
    pallas_call x1, Pallas kernels: 17.2 us -> 18.9 us  [gather_points(): pl.pallas_call(functools.partial(gather_kernel, count, mesh.shape['feat']...]
    pallas_call x1, Pallas kernels: 25.7 us -> 25 us  [shards(): pl.pallas_call(factor_kernel, grid=(tiles,), out_shape=(jax.ShapeDtypeStr...]
where the time goes in v2:
time: 44.7 us; the launch traced here: 44.5 us
  Pallas kernels  43.9 us (98%)
  between operations  0.64 us (1%)
    pallas_call x1, Pallas kernels, shards(): pl.pallas_call(factor_kernel, grid=(tiles,), out_shape=(jax.ShapeDtypeStr...  25 us
    pallas_call x1, Pallas kernels, gather_points(): pl.pallas_call(functools.partial(gather_kernel, count, mesh.shape['feat']...  18.9 us

profile of v2, /device:TPU:0, one launch (start us, length us, event | category | flops | bytes accessed | tf_op | source)
XLA Modules:
  0.0 44.5 jit_solution(1319966331916663120)
XLA Ops:
  0.6 18.9 %shard_map.41 = f32[16,16,128]{2,1,0:T(8,128)} custom-call(s32[2,128]{1,0:T(2,128)} %pivots.1, f32[8192,128]{1,0:T(8,128)} %frames.3), custom_call_target="tpu_custom_call" | custom-call | tf_op jit(solution)/shard_map/pallas_call | solution.py:114
  19.6 25.0 %shard_map.42 = (f32[8192,256]{1,0:T(8,128)}, f32[8,1,1024]{2,1,0:T(1,128)}) custom-call(f32[256,128]{1,0:T(8,128)} %bitcast.2, f32[8192,128]{1,0:T(8,128)} %frames.3), custom_call_target="tpu_custom_call" | custom-call | tf_op jit(solution)/shard_map/pallas_call | solution.py:252

commit v3 on v2

--- a/solution.py
+++ b/solution.py
@@ -11,7 +11,6 @@
 HIGHEST = lax.Precision.HIGHEST
 MESH = pl.DeviceIdType.MESH
 SUB = 8
-TILE = 1024
 
 
 def gather_kernel(count, feat_size, pivots, frames, points, held, mine, came, full, load_sem, s1, r1, s2, r2):
@@ -145,7 +144,7 @@
     return high, (value - high.astype(jnp.float32)).astype(jnp.bfloat16)
 
 
-def inverse_factor(matrix):
+def inverse_factor(matrix, beside):
     size = matrix.shape[0]
     rows = [matrix[i * SUB : (i + 1) * SUB, :] for i in range(size // SUB)]
     sub = lax.broadcasted_iota(jnp.int32, (SUB, size), 0)
@@ -174,6 +173,7 @@
             for m in range(j + 1, SUB):
                 pivot_col = row(cols[m], j)
                 cols[m] = jnp.where(sub == j, pivot_col * inverse, cols[m] - scaled * pivot_col)
+        beside(k)
         out.append(jnp.where(lane <= base + sub, done, 0.0))
         reduced = [row(work, j) for j in range(SUB)]
         for i in range(k + 1, size // SUB):
@@ -184,89 +184,155 @@
     return jnp.concatenate(out, axis=0)
 
 
-def factor_kernel(points, frames, factor, residual, pts, wt):
-    feat = points.shape[1]
-    slots = points.shape[0]
+def factor_kernel(
+    points, frames, factor, residual, held, pts, k_hi, k_lo, out1, out2, w_first, w_hi, w_lo,
+    load_sem, sem1, sem2,
+):
+    slots, feat = points.shape
     block = slots // 2
+    row_count = frames.shape[0]
+    chunks = block // SUB
+    chunk = row_count // chunks
+    half = row_count // 2
+    group = chunks // sem1.shape[0]
     fold = -0.5 / feat * math.log2(math.e)
 
-    @pl.when(pl.program_id(0) == 0)
-    def _():
-        table = points[...]
-        squares = table * table
-        ones = jnp.ones((SUB, feat), jnp.float32)
-        norms = fold * dot(ones, squares, ((1,), (1,)), HIGHEST)
-        products = dot(table, table, ((1,), (1,)), HIGHEST)
-        gram = jnp.exp2(
-            (fold * jnp.sum(squares, axis=1, keepdims=True) + norms[:1]) - 2.0 * fold * products
-        )
-        first = inverse_factor(gram[:block, :block])
-        earlier = dot(gram[block:, :block], first, ((1,), (1,)), HIGHEST)
-        second = inverse_factor(
-            gram[block:, block:] - dot(earlier, earlier, ((1,), (1,)), HIGHEST)
-        )
-        mixed = -dot(second, dot(earlier, first, precision=HIGHEST), precision=HIGHEST)
-        whole = jnp.concatenate(
-            [
-                jnp.concatenate([first, jnp.zeros_like(first)], axis=1),
-                jnp.concatenate([mixed, second], axis=1),
-            ],
-            axis=0,
-        ).T
-        high, low = halves(whole)
-        wt[...] = jnp.concatenate([high, high, low], axis=0)
-        high, low = halves((-2.0 * fold) * table.T)
-        n_high, n_rest = halves(norms)
-        rest = norms - n_high.astype(jnp.float32)
-        n_low = (rest - n_rest.astype(jnp.float32)).astype(jnp.bfloat16)
-        row = lax.broadcasted_iota(jnp.int32, (feat, slots), 0)
-        extra = jnp.where(
-            row == 0,
-            n_high[:1].astype(jnp.float32),
-            jnp.where(
-                row == 1,
-                n_rest[:1].astype(jnp.float32),
-                jnp.where(row == 2, n_low[:1].astype(jnp.float32), 0.0),
-            ),
-        ).astype(jnp.bfloat16)
-        pts[...] = jnp.concatenate([high, high, low, extra], axis=0)
-
-    tile = frames[...]
-    tile_norms = fold * jnp.sum(tile * tile, axis=1, keepdims=True)
-    high, low = halves(tile)
-    exponent = dot(
-        jnp.concatenate([high, low, high, jnp.ones_like(high)], axis=1), pts[...]
+    def load(part):
+        rows = pl.ds(part * half, half)
+        return pltpu.make_async_copy(frames.at[rows, :], held.at[rows, :], load_sem.at[part])
+
+    def store1(part):
+        rows = pl.ds(part * group * chunk, group * chunk)
+        return pltpu.make_async_copy(
+            out1.at[rows, :], factor.at[rows, pl.ds(0, block)], sem1.at[part]
+        )
+
+    def store2(part):
+        rows = pl.ds(part * chunk, chunk)
+        return pltpu.make_async_copy(
+            out2.at[rows, :], factor.at[rows, pl.ds(block, block)], sem2.at[part]
+        )
+
+    load(0).start()
+    load(1).start()
+
+    table = points[...]
+    squares = table * table
+    ones = jnp.ones((SUB, feat), jnp.float32)
+    norms = fold * dot(ones, squares, ((1,), (1,)), HIGHEST)
+    products = dot(table, table, ((1,), (1,)), HIGHEST)
+    gram = jnp.exp2(
+        (fold * jnp.sum(squares, axis=1, keepdims=True) + norms[:1]) - 2.0 * fold * products
     )
-    high, low = halves(jnp.exp2(tile_norms + exponent))
-    result = dot(jnp.concatenate([high, low, high], axis=1), wt[...])
-    factor[...] = result
-    squares = result[:, :block] * result[:, :block] + result[:, block:] * result[:, block:]
-    residual[0] = 1.0 - jnp.sum(squares.T, axis=0, keepdims=True)
+    high, low = halves((-2.0 * fold) * table.T)
+    n_high, n_rest = halves(norms)
+    rest = norms - n_high.astype(jnp.float32)
+    n_low = (rest - n_rest.astype(jnp.float32)).astype(jnp.bfloat16)
+    row = lax.broadcasted_iota(jnp.int32, (feat, slots), 0)
+    extra = jnp.where(
+        row == 0,
+        n_high[:1].astype(jnp.float32),
+        jnp.where(
+            row == 1,
+            n_rest[:1].astype(jnp.float32),
+            jnp.where(row == 2, n_low[:1].astype(jnp.float32), 0.0),
+        ),
+    ).astype(jnp.bfloat16)
+    pts[...] = jnp.concatenate([high, high, low, extra], axis=0)
+    load(0).wait()
+
+    def kern_chunk(k):
+        if k == chunks // 2:
+            load(1).wait()
+        rows = pl.ds(k * chunk, chunk)
+        tile = held[rows, :]
+        tile_norms = fold * jnp.sum(tile * tile, axis=1, keepdims=True)
+        high, low = halves(tile)
+        exponent = dot(
+            jnp.concatenate([high, low, high, jnp.ones_like(high)], axis=1), pts[...]
+        )
+        high, low = halves(jnp.exp2(tile_norms + exponent))
+        k_hi[rows, :] = high
+        k_lo[rows, :] = low
+
+    first = inverse_factor(gram[:block, :block], kern_chunk)
+    earlier = dot(gram[block:, :block], first, ((1,), (1,)), HIGHEST)
+    schur = gram[block:, block:] - dot(earlier, earlier, ((1,), (1,)), HIGHEST)
+    high, low = halves(first.T)
+    w_first[...] = jnp.concatenate(
+        [
+            jnp.concatenate([high, low], axis=1),
+            jnp.concatenate([high, jnp.zeros_like(high)], axis=1),
+        ],
+        axis=0,
+    )
+    carried = dot(earlier, first, precision=HIGHEST)
+
+    def first_chunk(k):
+        rows = pl.ds(k * chunk, chunk)
+        both = jnp.concatenate([k_hi[rows, :block], k_lo[rows, :block]], axis=1)
+        result = dot(both, w_first[...])
+        out1[rows, :] = result[:, :block] + result[:, block:]
+        if k % group == group - 1:
+            store1(k // group).start()
+
+    second = inverse_factor(schur, first_chunk)
+    mixed = -dot(second, carried, precision=HIGHEST)
+    high, low = halves(jnp.concatenate([mixed, second], axis=1).T)
+    w_hi[...] = jnp.concatenate([high, low], axis=1)
+    w_lo[...] = high
+
+    def second_chunk(k, carry):
+        rows = pl.ds(pl.multiple_of(k * chunk, chunk), chunk)
+        wide = dot(k_hi[rows, :], w_hi[...])
+        result = wide[:, :block] + wide[:, block:] + dot(k_lo[rows, :], w_lo[...])
+        out2[rows, :] = result
+        store2(k).start()
+        before = out1[rows, :]
+        squares = before * before + result * result
+        residual[k] = 1.0 - jnp.sum(squares.T, axis=0, keepdims=True)
+        return carry
+
+    lax.fori_loop(0, chunks, second_chunk, 0)
+    for k in range(chunks // group):
+        store1(k).wait()
+
+    def finish(k, carry):
+        store2(k).wait()
+        return carry
+
+    lax.fori_loop(0, chunks, finish, 0)
 
 
 def shards(mesh, frames, pivots):
     points = gather_points(mesh, frames, pivots)
     row_count, feat = frames.shape
     slots = points.shape[0]
-    tiles = row_count // TILE
+    block = slots // 2
+    chunks = block // SUB
+    vmem = pl.BlockSpec(memory_space=pltpu.VMEM)
+    anywhere = pl.BlockSpec(memory_space=pl.ANY)
     factor, residual = pl.pallas_call(
         factor_kernel,
-        grid=(tiles,),
         out_shape=(
             jax.ShapeDtypeStruct((row_count, slots), jnp.float32),
-            jax.ShapeDtypeStruct((tiles, 1, TILE), jnp.float32),
+            jax.ShapeDtypeStruct((chunks, 1, row_count // chunks), jnp.float32),
         ),
-        in_specs=[
-            pl.BlockSpec((slots, feat), lambda i: (0, 0)),
-            pl.BlockSpec((TILE, feat), lambda i: (i, 0)),
-        ],
-        out_specs=(
-            pl.BlockSpec((TILE, slots), lambda i: (i, 0)),
-            pl.BlockSpec((1, 1, TILE), lambda i: (i, 0, 0)),
-        ),
+        in_specs=[vmem, anywhere],
+        out_specs=(anywhere, vmem),
         scratch_shapes=[
+            pltpu.VMEM((row_count, feat), jnp.float32),
             pltpu.VMEM((4 * feat, slots), jnp.bfloat16),
-            pltpu.VMEM((3 * slots, slots), jnp.bfloat16),
+            pltpu.VMEM((row_count, slots), jnp.bfloat16),
+            pltpu.VMEM((row_count, slots), jnp.bfloat16),
+            pltpu.VMEM((row_count, block), jnp.float32),
+            pltpu.VMEM((row_count, block), jnp.float32),
+            pltpu.VMEM((slots, slots), jnp.bfloat16),
+            pltpu.VMEM((slots, slots), jnp.bfloat16),
+            pltpu.VMEM((slots, block), jnp.bfloat16),
+            pltpu.SemaphoreType.DMA((2,)),
+            pltpu.SemaphoreType.DMA((4,)),
+            pltpu.SemaphoreType.DMA((chunks,)),
         ],
         compiler_params=pltpu.CompilerParams(vmem_limit_bytes=60 * 1024 * 1024),
     )(points, frames)

time: 44.7 us -> 40.9 us (0.915)
  Pallas kernels: 43.9 us -> 40 us
    pallas_call x1, Pallas kernels: 25 us -> 21.1 us  [shards(): pl.pallas_call(factor_kernel, out_shape=(jax.ShapeDtypeStruct((row_count,...]
where the time goes in v3:
time: 40.9 us; the launch traced here: 40.7 us
  Pallas kernels  40 us (98%)
  between operations  0.64 us (2%)
    pallas_call x1, Pallas kernels, shards(): pl.pallas_call(factor_kernel, out_shape=(jax.ShapeDtypeStruct((row_count,...  21.1 us
    pallas_call x1, Pallas kernels, gather_points(): pl.pallas_call(functools.partial(gather_kernel, count, mesh.shape['feat']...  18.9 us

profile of v3, /device:TPU:0, one launch (start us, length us, event | category | flops | bytes accessed | tf_op | source)
XLA Modules:
  0.0 40.7 jit_solution(12528458690012927298)
XLA Ops:
  0.6 18.9 %shard_map.41 = f32[16,16,128]{2,1,0:T(8,128)} custom-call(s32[2,128]{1,0:T(2,128)} %pivots.1, f32[8192,128]{1,0:T(8,128)} %frames.3), custom_call_target="tpu_custom_call" | custom-call | tf_op jit(solution)/shard_map/pallas_call | solution.py:113
  19.6 21.1 %shard_map.42 = (f32[8192,256]{1,0:T(8,128)}, f32[16,1,512]{2,1,0:T(1,128)}) custom-call(f32[256,128]{1,0:T(8,128)} %bitcast.2, f32[8192,128]{1,0:T(8,128)} %frames.3), custom_call_target="tpu_custom_call" | custom-call | tf_op jit(solution)/shard_map/pallas_call | solution.py:315

commit v4 on v3

--- a/solution.py
+++ b/solution.py
@@ -20,8 +20,15 @@
     share = mine.shape[1]
     block = pivots.shape[1]
 
-    load = pltpu.make_async_copy(frames, held, load_sem)
-    load.start()
+    parts = load_sem.shape[0]
+    loads = []
+    for part in range(parts):
+        rows = pl.ds(part * (row_count // parts), row_count // parts)
+        loads.append(
+            pltpu.make_async_copy(frames.at[rows, :], held.at[rows, :], load_sem.at[part])
+        )
+    for load in loads:
+        load.start()
 
     def device(index):
         return {"dp": index // feat_size, "feat": index % feat_size}
@@ -34,18 +41,17 @@
         return carry
 
     lax.fori_loop(1, count, greet, 0)
-    load.wait()
-
-    def pick(owner, carry):
+    for load in loads:
+        load.wait()
+
+    def pick(owner):
         for k in range(share):
             slot = owner * share + k
             local = pivots[slot // block, slot % block] - start
             is_mine = (local >= 0) & (local < row_count)
             row = held[pl.ds(jnp.clip(local, 0, row_count - 1), 1), :]
             mine[owner, pl.ds(k, 1), :] = row * jnp.where(is_mine, 1.0, 0.0)
-        return carry
-
-    lax.fori_loop(0, count, pick, 0)
+
     pl.semaphore_wait(barrier, count - 1)
 
     def collect(step):
@@ -88,7 +94,12 @@
 
         lax.fori_loop(1, count, body, 0)
 
-    run(lambda step: collect(step).start())
+    def send(step):
+        pick(lax.rem(me + step, count))
+        collect(step).start()
+
+    run(send)
+    pick(me)
 
     def add(step, total):
         collect(step).wait_recv()
@@ -120,7 +131,7 @@
             pltpu.VMEM(table, jnp.float32),
             pltpu.VMEM(table, jnp.float32),
             pltpu.VMEM(table, jnp.float32),
-            pltpu.SemaphoreType.DMA(()),
+            pltpu.SemaphoreType.DMA((8,)),
             sems,
             sems,
             sems,
@@ -168,11 +179,11 @@
             inverse = 1.0 / pivot
             pivot_row = row(work, j)
             done = jnp.where(sub == j, pivot_row * lax.rsqrt(pivot), done)
-            scaled = cols[j] * inverse
-            work = jnp.where(sub == j, pivot_row * inverse, work - scaled * pivot_row)
+            weight = jnp.where(sub == j, pivot - 1.0, cols[j])
+            work = work - (weight * pivot_row) * inverse
             for m in range(j + 1, SUB):
                 pivot_col = row(cols[m], j)
-                cols[m] = jnp.where(sub == j, pivot_col * inverse, cols[m] - scaled * pivot_col)
+                cols[m] = cols[m] - (weight * pivot_col) * inverse
         beside(k)
         out.append(jnp.where(lane <= base + sub, done, 0.0))
         reduced = [row(work, j) for j in range(SUB)]
@@ -293,7 +304,7 @@
         residual[k] = 1.0 - jnp.sum(squares.T, axis=0, keepdims=True)
         return carry
 
-    lax.fori_loop(0, chunks, second_chunk, 0)
+    lax.fori_loop(0, chunks, second_chunk, 0, unroll=4)
     for k in range(chunks // group):
         store1(k).wait()
 

time: 40.9 us -> 37.1 us (0.907)
  Pallas kernels: 40 us -> 36.3 us
    pallas_call x1, Pallas kernels: 21.1 us -> 17.6 us  [shards(): pl.pallas_call(factor_kernel, out_shape=(jax.ShapeDtypeStruct((row_count,...]
where the time goes in v4:
time: 37.1 us; the launch traced here: 36.9 us
  Pallas kernels  36.3 us (98%)
  between operations  0.64 us (2%)
    pallas_call x1, Pallas kernels, gather_points(): pl.pallas_call(functools.partial(gather_kernel, count, mesh.shape['feat']...  18.7 us
    pallas_call x1, Pallas kernels, shards(): pl.pallas_call(factor_kernel, out_shape=(jax.ShapeDtypeStruct((row_count,...  17.6 us

profile of v4, /device:TPU:0, one launch (start us, length us, event | category | flops | bytes accessed | tf_op | source)
XLA Modules:
  0.0 36.9 jit_solution(5976604820985679482)
XLA Ops:
  0.6 18.7 %shard_map.41 = f32[16,16,128]{2,1,0:T(8,128)} custom-call(s32[2,128]{1,0:T(2,128)} %pivots.1, f32[8192,128]{1,0:T(8,128)} %frames.3), custom_call_target="tpu_custom_call" | custom-call | tf_op jit(solution)/shard_map/pallas_call | solution.py:124
  19.3 17.6 %shard_map.42 = (f32[8192,256]{1,0:T(8,128)}, f32[16,1,512]{2,1,0:T(1,128)}) custom-call(f32[256,128]{1,0:T(8,128)} %bitcast.2, f32[8192,128]{1,0:T(8,128)} %frames.3), custom_call_target="tpu_custom_call" | custom-call | tf_op jit(solution)/shard_map/pallas_call | solution.py:326
